TPU v7x, 32 devices: a whole 2x2x4 slice. The times are simulated.
32 devices in a mesh: ctx: 8 (over y, x, core), fsdp: 4 (over z).
Axes of the slice: x: 2, y: 2, z: 4, core: 2. Of those that a mesh axis runs over, the one named last changes fastest.
Arguments:
- hidden: bfloat16 [4, 2048, 4096], P('fsdp', 'ctx'), may hold values from -6 to 6
- queries: bfloat16 [4, 2048, 2048], P('fsdp', 'ctx'), may hold values from -6 to 6
- key_weight: bfloat16 [4096, 512], P('fsdp'), may hold values from -0.09375 to 0.09375
- value_weight: bfloat16 [4096, 512], P('fsdp'), may hold values from -0.09375 to 0.09375
- key_gain: float32 [128], replicated, may hold values from 0.7 to 1.3
- head_scale: float32 [16], replicated, may hold values from 1 to 4
- block_mask: int32 [4, 16, 16], P('fsdp', 'ctx'), may hold values from 0 to 1, as said below
Outputs:
- attended: bfloat16 [4, 2048, 2048], P('fsdp', 'ctx')
Inputs may be any that keep to these rules, and one draw needn't show every extreme that they name: `block_mask`: in each sequence's table, entry (q, k) is 1 where k == q, 0 where k > q, and either 0 or 1 where k < q.
All inputs are finite; a program needn't handle non-finite values.
Results may differ from a plain program's by a relative error of at most 0.011.
Values may be sent and summed in bfloat16 or wider, within the bound.
A program may use at most 64 MiB of HBM per device.

v0:
```python
import math

import jax
import jax.numpy as jnp
from jax import lax
from jax.sharding import PartitionSpec as P


def shifted(value, axis, steps):
    count = lax.axis_size(axis)
    leading, last = (max(0, -steps), min(count, count - steps))
    return lax.ppermute(value, axis, [(source, source + steps) for source in range(leading, last)])


def rms_scale(vecs):
    return vecs * lax.rsqrt(jnp.mean(vecs * vecs, axis=-1, keepdims=True) + 1e-06)


def shards(hidden, queries, key_weight, value_weight, key_gain, head_scale, block_mask):
    seq_dev, local_len, model_width = hidden.shape
    kv_width = key_weight.shape[1]
    head_dim = key_gain.shape[0]
    head_count = head_scale.shape[0]
    kv_heads = kv_width // head_dim
    groups = head_count // kv_heads
    frames = block_mask.shape[1]
    frame_len = local_len // frames
    flat_rows = hidden.reshape(seq_dev * local_len, model_width)

    def add_rows(piece):
        return jnp.dot(flat_rows, piece, preferred_element_type=jnp.float32)

    key_sums = add_rows(lax.all_gather(key_weight, "fsdp", axis=0, tiled=True))
    value_sums = add_rows(lax.all_gather(value_weight, "fsdp", axis=0, tiled=True))
    key_vecs = rms_scale(key_sums.reshape(seq_dev, local_len, kv_heads, head_dim)) * key_gain
    key_vecs = key_vecs.astype(jnp.bfloat16)
    value_vecs = value_sums.astype(jnp.bfloat16).reshape(seq_dev, local_len, kv_heads, head_dim)
    stacked = jnp.stack([key_vecs, value_vecs])
    head_factor = (head_scale / math.sqrt(head_dim)).reshape(1, 1, kv_heads, groups, 1)
    scaled_q = (
        rms_scale(
            queries.astype(jnp.float32).reshape(seq_dev, local_len, kv_heads, groups, head_dim)
        )
        * head_factor
    )
    scaled_q = scaled_q.astype(jnp.bfloat16)

    def attend_when(sums, kv_piece, start, usable):
        key_piece = kv_piece[0]
        value_piece = kv_piece[1]
        piece_len = key_piece.shape[1]
        key_frames = piece_len // frame_len
        allow_table = lax.dynamic_slice_in_dim(block_mask, start // frame_len, key_frames, 2)

        def accumulate(current):
            numer, denom = current
            scores = jnp.einsum(
                "bqkgd,bpkd->bkgqp", scaled_q, key_piece, preferred_element_type=jnp.float32
            )
            allowed = jnp.broadcast_to(
                allow_table[:, :, None, :, None] > 0,
                (seq_dev, frames, frame_len, key_frames, frame_len),
            )
            allowed = allowed.reshape(seq_dev, local_len, piece_len)
            weights = jnp.where(allowed[:, None, None], jnp.exp(scores), jnp.float32(0.0))
            denom = denom + jnp.sum(weights, axis=-1)
            numer = numer + jnp.einsum(
                "bkgqp,bpkd->bkgqd",
                weights.astype(jnp.bfloat16),
                value_piece,
                preferred_element_type=jnp.float32,
            )
            return (numer, denom)

        def unchanged(current):
            return current

        return lax.cond(
            jnp.logical_and(usable, jnp.any(allow_table > 0)), accumulate, unchanged, sums
        )

    start_sums = (
        jnp.zeros((seq_dev, kv_heads, groups, local_len, head_dim), jnp.float32),
        jnp.zeros((seq_dev, kv_heads, groups, local_len), jnp.float32),
    )
    ctx_count = lax.axis_size("ctx")
    own_index = lax.axis_index("ctx")
    result = attend_when(start_sums, stacked, own_index * local_len, jnp.bool_(True))

    def relay_step(step_no, carried):
        sums, moving = carried
        moving = shifted(moving, "ctx", 1)
        anchor = own_index - step_no
        usable = anchor >= 0
        safe_anchor = jnp.maximum(anchor, 0)
        return (attend_when(sums, moving, safe_anchor * local_len, usable), moving)

    result = lax.fori_loop(1, ctx_count, relay_step, (result, stacked))[0]
    numer, denom = result
    attended = numer / denom[..., None]
    attended = attended.transpose(0, 3, 1, 2, 4).reshape(seq_dev, local_len, head_count * head_dim)
    return attended.astype(jnp.bfloat16)


def solution(mesh):
    placed = (
        P("fsdp", "ctx", None),
        P("fsdp", "ctx", None),
        P("fsdp", None),
        P("fsdp", None),
        P(),
        P(),
        P("fsdp", "ctx", None),
    )
    return jax.shard_map(
        shards, mesh=mesh, in_specs=placed, out_specs=P("fsdp", "ctx", None), check_vma=False
    )
```

profile of v0, /device:TPU:15, one launch (start us, length us, event | category | flops | bytes accessed | tf_op | source)
XLA Modules:
  0.0 317.4 jit_solution(3327830303517072997)
XLA Ops:
  12.6 2.3 copy.54
  14.9 73.4 %all-gather.3.cloned.1.call-done = bf16[4096,512]{1,0:T(8,128)(2,1)} async-done(((bf16[1024,512]{1,0:T(8,128)(2,1)}), bf16[4096,512]{1,0:T(8,128)(2,1)}) %all-gather.3.cloned.1.call-update) | async-done | bytes 4194320 | tf_op jit(solution)/shard_map/all_gather | solution.py:33
  88.4 3.4 %fusion.36 = f32[256,512]{1,0:T(8,128)S(1)} fusion(bf16[4096,512]{1,0:T(8,128)(2,1)} %all-gather.3.cloned.1.call-done, bf16[1,256,4096]{2,1,0:T(8,128)(2,1)S(1)} %copy-done), kind=kOutput, calls=%fused_computation.42 | convolution fusion | flops 1073741824 | bytes 6815744 | tf_op jit(solution)/shard_map/dot_general | solution.py:31
  95.6 73.7 %all-gather.5.cloned.1.call-done = bf16[4096,512]{1,0:T(8,128)(2,1)} async-done(((bf16[1024,512]{1,0:T(8,128)(2,1)}), bf16[4096,512]{1,0:T(8,128)(2,1)}) %all-gather.5.cloned.1.call-update) | async-done | bytes 4194320 | tf_op jit(solution)/shard_map/all_gather | solution.py:34
  169.3 4.1 %fusion.38 = bf16[256,512]{1,0:T(8,128)(2,1)} fusion(bf16[4096,512]{1,0:T(8,128)(2,1)} %all-gather.5.cloned.1.call-done, bf16[1,256,4096]{2,1,0:T(8,128)(2,1)S(1)} %copy-done), kind=kOutput, calls=%fused_computation.45 | convolution fusion | flops 1073872896 | bytes 6553600 | tf_op jit(solution)/shard_map/dot_general | solution.py:31
  177.9 8.7 %conditional.2 = (f32[1,4,4,256,128]{4,3,2,1,0:T(8,128)}, f32[1,4,4,256]{3,2,1,0:T(4,128)S(1)}) conditional(s32[]{:T(128)} %convert_element_type.71, () %tuple.42, (s32[1,2,2]{2,1,0:T(2,128)S(1)}, bf16[1,256,4,128]{3,1,2,0:T(8,128)(2,1)S(1)}, bf16[1,256,4,4,128]{1,4,3,2,0:T(8,128)(2,1)S(1)}, bf16[256,512]{1,0:T(8,128)(2,1)}) %tuple.82), branch_computations={%region_3.4_spmd, %region_4.6_spmd} | conditional | flops 541061120 | bytes 13058088 | solution.py:78
  178.3 2.7 fusion
  182.0 4.6 %fusion.7 = f32[1,4,4,256,128]{4,3,2,1,0:T(8,128)} fusion(f32[4,256,256,4]{2,1,3,0:T(8,128)} %get-tuple-element.290, pred[256,256]{0,1:T(8,128)(4,1)S(1)} %copy.43, bf16[256,4,128,1]{2,1,0,3:T(4,128)(2,1)S(1)} %bitcast.111), kind=kOutput, calls=%fused_computation.7 | convolution fusion | flops 270532608 | bytes 6619136 | tf_op jit(solution)/shard_map/cond/branch_1_fun/bkgqp,bpkd->bkgqd/dot_general | solution.py:67
  186.6 119.6 %while.19 = (s32[]{:T(128)}, f32[1,4,4,256,128]{4,3,2,1,0:T(8,128)}, f32[1,4,4,256]{3,2,1,0:T(4,128)S(1)}, bf16[2,1,256,4,128]{4,2,3,1,0:T(8,128)(2,1)}, s32[]{:...) while((s32[]{:T(128)}, ...), condition=%wide.region_11.12_spmd, body=%wide.region_6.11_spmd.sunk | while | flops 541589504 | bytes 17826344 | solution.py:98
  190.8 6.5 %conditional.4 = ((f32[1,4,4,256,128]{4,3,2,1,0:T(8,128)}, f32[1,4,4,256]{3,2,1,0:T(4,128)S(1)})) conditional(s32[]{:T(128)} %convert_element_type.99, (f32[1,4,4,256,128]{4,3,2,1,0:T(8,128)}, f32[1,4,4,256]{3,2,1,0:T(4,128)S(1)}) %tuple.67, (s32[1,2,2]{2,1,0:T(2,128)S(1)}, bf16[2,1,256,4,128]{4,2,3,1,0:T(8,128)(2,1)S(1)}, ...), branch_computations={%region_8.8_spmd, %region_9.10_spmd} | conditional | flops 541589504 | bytes 14680112 | solution.py:78
  191.1 2.1 fusion.15
  193.3 4.0 %bitcast_add_fusion = f32[1,4,4,256,128]{4,3,2,1,0:T(8,128)} fusion(f32[1,4,4,256,128]{4,3,2,1,0:T(8,128)} %get-tuple-element.215, f32[4,256,256,4]{2,1,3,0:T(8,128)S(1)} %get-tuple-element.292, pred[256,256]{0,1:T(8,128)(4,1)S(1)} %copy.46, bf16[2,1,256,4,128]{4,2,3,1,0:T(8,128)(2,1)S(1)} %get-tuple-element.217), kind=kOutput, calls=%fused_computation.20 | convolution fusion | flops 271056896 | bytes 8716288 | tf_op jit(solution)/shard_map/while/body/eval_jaxpr/cond/branch_1_fun/bkgqp,bpkd->bkgqd/dot_general | solution.py:67
  201.5 7.3 %collective-permute-done = bf16[2,1,256,4,128]{4,2,3,1,0:T(8,128)(2,1)S(1)} collective-permute-done((bf16[2,1,256,4,128]{4,2,3,1,0:T(8,128)(2,1)}, bf16[2,1,256,4,128]{4,2,3,1,0:T(8,128)(2,1)S(1)}, u32[]{:S(2)}, u32[]{:S(2)}) %collective-permute-start) | collective-permute-done | bytes 524320 | tf_op jit(solution)/shard_map/while/body/eval_jaxpr/ppermute | solution.py:12
  213.0 13.8 %collective-permute-done = bf16[2,1,256,4,128]{4,2,3,1,0:T(8,128)(2,1)S(1)} collective-permute-done((bf16[2,1,256,4,128]{4,2,3,1,0:T(8,128)(2,1)}, bf16[2,1,256,4,128]{4,2,3,1,0:T(8,128)(2,1)S(1)}, u32[]{:S(2)}, u32[]{:S(2)}) %collective-permute-start) | collective-permute-done | bytes 524320 | tf_op jit(solution)/shard_map/while/body/eval_jaxpr/ppermute | solution.py:12
  226.8 6.5 %conditional.4 = ((f32[1,4,4,256,128]{4,3,2,1,0:T(8,128)}, f32[1,4,4,256]{3,2,1,0:T(4,128)S(1)})) conditional(s32[]{:T(128)} %convert_element_type.99, (f32[1,4,4,256,128]{4,3,2,1,0:T(8,128)}, f32[1,4,4,256]{3,2,1,0:T(4,128)S(1)}) %tuple.67, (s32[1,2,2]{2,1,0:T(2,128)S(1)}, bf16[2,1,256,4,128]{4,2,3,1,0:T(8,128)(2,1)S(1)}, ...), branch_computations={%region_8.8_spmd, %region_9.10_spmd} | conditional | flops 541589504 | bytes 14680112 | solution.py:78
  227.2 2.1 fusion.15
  229.3 4.0 %bitcast_add_fusion = f32[1,4,4,256,128]{4,3,2,1,0:T(8,128)} fusion(f32[1,4,4,256,128]{4,3,2,1,0:T(8,128)} %get-tuple-element.215, f32[4,256,256,4]{2,1,3,0:T(8,128)S(1)} %get-tuple-element.292, pred[256,256]{0,1:T(8,128)(4,1)S(1)} %copy.46, bf16[2,1,256,4,128]{4,2,3,1,0:T(8,128)(2,1)S(1)} %get-tuple-element.217), kind=kOutput, calls=%fused_computation.20 | convolution fusion | flops 271056896 | bytes 8716288 | tf_op jit(solution)/shard_map/while/body/eval_jaxpr/cond/branch_1_fun/bkgqp,bpkd->bkgqd/dot_general | solution.py:67
  237.5 7.3 %collective-permute-done = bf16[2,1,256,4,128]{4,2,3,1,0:T(8,128)(2,1)S(1)} collective-permute-done((bf16[2,1,256,4,128]{4,2,3,1,0:T(8,128)(2,1)}, bf16[2,1,256,4,128]{4,2,3,1,0:T(8,128)(2,1)S(1)}, u32[]{:S(2)}, u32[]{:S(2)}) %collective-permute-start) | collective-permute-done | bytes 524320 | tf_op jit(solution)/shard_map/while/body/eval_jaxpr/ppermute | solution.py:12
  244.8 6.5 %conditional.4 = ((f32[1,4,4,256,128]{4,3,2,1,0:T(8,128)}, f32[1,4,4,256]{3,2,1,0:T(4,128)S(1)})) conditional(s32[]{:T(128)} %convert_element_type.99, (f32[1,4,4,256,128]{4,3,2,1,0:T(8,128)}, f32[1,4,4,256]{3,2,1,0:T(4,128)S(1)}) %tuple.67, (s32[1,2,2]{2,1,0:T(2,128)S(1)}, bf16[2,1,256,4,128]{4,2,3,1,0:T(8,128)(2,1)S(1)}, ...), branch_computations={%region_8.8_spmd, %region_9.10_spmd} | conditional | flops 541589504 | bytes 14680112 | solution.py:78
  245.2 2.1 fusion.15
  247.3 4.0 %bitcast_add_fusion = f32[1,4,4,256,128]{4,3,2,1,0:T(8,128)} fusion(f32[1,4,4,256,128]{4,3,2,1,0:T(8,128)} %get-tuple-element.215, f32[4,256,256,4]{2,1,3,0:T(8,128)S(1)} %get-tuple-element.292, pred[256,256]{0,1:T(8,128)(4,1)S(1)} %copy.46, bf16[2,1,256,4,128]{4,2,3,1,0:T(8,128)(2,1)S(1)} %get-tuple-element.217), kind=kOutput, calls=%fused_computation.20 | convolution fusion | flops 271056896 | bytes 8716288 | tf_op jit(solution)/shard_map/while/body/eval_jaxpr/cond/branch_1_fun/bkgqp,bpkd->bkgqd/dot_general | solution.py:67
  255.5 7.3 %collective-permute-done = bf16[2,1,256,4,128]{4,2,3,1,0:T(8,128)(2,1)S(1)} collective-permute-done((bf16[2,1,256,4,128]{4,2,3,1,0:T(8,128)(2,1)}, bf16[2,1,256,4,128]{4,2,3,1,0:T(8,128)(2,1)S(1)}, u32[]{:S(2)}, u32[]{:S(2)}) %collective-permute-start) | collective-permute-done | bytes 524320 | tf_op jit(solution)/shard_map/while/body/eval_jaxpr/ppermute | solution.py:12
  262.8 6.5 %conditional.4 = ((f32[1,4,4,256,128]{4,3,2,1,0:T(8,128)}, f32[1,4,4,256]{3,2,1,0:T(4,128)S(1)})) conditional(s32[]{:T(128)} %convert_element_type.99, (f32[1,4,4,256,128]{4,3,2,1,0:T(8,128)}, f32[1,4,4,256]{3,2,1,0:T(4,128)S(1)}) %tuple.67, (s32[1,2,2]{2,1,0:T(2,128)S(1)}, bf16[2,1,256,4,128]{4,2,3,1,0:T(8,128)(2,1)S(1)}, ...), branch_computations={%region_8.8_spmd, %region_9.10_spmd} | conditional | flops 541589504 | bytes 14680112 | solution.py:78
  263.2 2.1 fusion.15
  265.3 4.0 %bitcast_add_fusion = f32[1,4,4,256,128]{4,3,2,1,0:T(8,128)} fusion(f32[1,4,4,256,128]{4,3,2,1,0:T(8,128)} %get-tuple-element.215, f32[4,256,256,4]{2,1,3,0:T(8,128)S(1)} %get-tuple-element.292, pred[256,256]{0,1:T(8,128)(4,1)S(1)} %copy.46, bf16[2,1,256,4,128]{4,2,3,1,0:T(8,128)(2,1)S(1)} %get-tuple-element.217), kind=kOutput, calls=%fused_computation.20 | convolution fusion | flops 271056896 | bytes 8716288 | tf_op jit(solution)/shard_map/while/body/eval_jaxpr/cond/branch_1_fun/bkgqp,bpkd->bkgqd/dot_general | solution.py:67
  273.5 7.3 %collective-permute-done = bf16[2,1,256,4,128]{4,2,3,1,0:T(8,128)(2,1)S(1)} collective-permute-done((bf16[2,1,256,4,128]{4,2,3,1,0:T(8,128)(2,1)}, bf16[2,1,256,4,128]{4,2,3,1,0:T(8,128)(2,1)S(1)}, u32[]{:S(2)}, u32[]{:S(2)}) %collective-permute-start) | collective-permute-done | bytes 524320 | tf_op jit(solution)/shard_map/while/body/eval_jaxpr/ppermute | solution.py:12
  280.8 6.5 %conditional.4 = ((f32[1,4,4,256,128]{4,3,2,1,0:T(8,128)}, f32[1,4,4,256]{3,2,1,0:T(4,128)S(1)})) conditional(s32[]{:T(128)} %convert_element_type.99, (f32[1,4,4,256,128]{4,3,2,1,0:T(8,128)}, f32[1,4,4,256]{3,2,1,0:T(4,128)S(1)}) %tuple.67, (s32[1,2,2]{2,1,0:T(2,128)S(1)}, bf16[2,1,256,4,128]{4,2,3,1,0:T(8,128)(2,1)S(1)}, ...), branch_computations={%region_8.8_spmd, %region_9.10_spmd} | conditional | flops 541589504 | bytes 14680112 | solution.py:78
  283.3 4.0 %bitcast_add_fusion = f32[1,4,4,256,128]{4,3,2,1,0:T(8,128)} fusion(f32[1,4,4,256,128]{4,3,2,1,0:T(8,128)} %get-tuple-element.215, f32[4,256,256,4]{2,1,3,0:T(8,128)S(1)} %get-tuple-element.292, pred[256,256]{0,1:T(8,128)(4,1)S(1)} %copy.46, bf16[2,1,256,4,128]{4,2,3,1,0:T(8,128)(2,1)S(1)} %get-tuple-element.217), kind=kOutput, calls=%fused_computation.20 | convolution fusion | flops 271056896 | bytes 8716288 | tf_op jit(solution)/shard_map/while/body/eval_jaxpr/cond/branch_1_fun/bkgqp,bpkd->bkgqd/dot_general | solution.py:67
  291.6 7.3 %collective-permute-done = bf16[2,1,256,4,128]{4,2,3,1,0:T(8,128)(2,1)S(1)} collective-permute-done((bf16[2,1,256,4,128]{4,2,3,1,0:T(8,128)(2,1)}, bf16[2,1,256,4,128]{4,2,3,1,0:T(8,128)(2,1)S(1)}, u32[]{:S(2)}, u32[]{:S(2)}) %collective-permute-start) | collective-permute-done | bytes 524320 | tf_op jit(solution)/shard_map/while/body/eval_jaxpr/ppermute | solution.py:12
  298.8 6.5 %conditional.4 = ((f32[1,4,4,256,128]{4,3,2,1,0:T(8,128)}, f32[1,4,4,256]{3,2,1,0:T(4,128)S(1)})) conditional(s32[]{:T(128)} %convert_element_type.99, (f32[1,4,4,256,128]{4,3,2,1,0:T(8,128)}, f32[1,4,4,256]{3,2,1,0:T(4,128)S(1)}) %tuple.67, (s32[1,2,2]{2,1,0:T(2,128)S(1)}, bf16[2,1,256,4,128]{4,2,3,1,0:T(8,128)(2,1)S(1)}, ...), branch_computations={%region_8.8_spmd, %region_9.10_spmd} | conditional | flops 541589504 | bytes 14680112 | solution.py:78
  299.2 2.1 fusion.15
  301.4 4.0 %bitcast_add_fusion = f32[1,4,4,256,128]{4,3,2,1,0:T(8,128)} fusion(f32[1,4,4,256,128]{4,3,2,1,0:T(8,128)} %get-tuple-element.215, f32[4,256,256,4]{2,1,3,0:T(8,128)S(1)} %get-tuple-element.292, pred[256,256]{0,1:T(8,128)(4,1)S(1)} %copy.46, bf16[2,1,256,4,128]{4,2,3,1,0:T(8,128)(2,1)S(1)} %get-tuple-element.217), kind=kOutput, calls=%fused_computation.20 | convolution fusion | flops 271056896 | bytes 8716288 | tf_op jit(solution)/shard_map/while/body/eval_jaxpr/cond/branch_1_fun/bkgqp,bpkd->bkgqd/dot_general | solution.py:67
  (95 shorter events, 49.2 us)
Async XLA Ops:
  6.5 81.8 %copy-start = (bf16[1,256,4096]{2,1,0:T(8,128)(2,1)S(1)}, bf16[1,256,4096]{2,1,0:T(8,128)(2,1)}, u32[]{:S(2)}) copy-start(bf16[1,256,4096]{2,1,0:T(8,128)(2,1)} %param.13) | copy-start | bytes 6291460
  6.5 3.0 copy-start.5
  6.5 3.1 copy-start.3
  6.5 81.8 %all-gather.3.cloned.1.call-start = ((), (), s32[]{:S(2)}) async-start(), calls=%async_computation | async-start | bytes 5242880 | tf_op jit(solution)/shard_map/all_gather | solution.py:33
  7.3 162.0 %all-gather.5.cloned.1.call-start = ((), (), s32[]{:S(2)}) async-start(), calls=%async_computation.1 | async-start | bytes 5242880 | tf_op jit(solution)/shard_map/all_gather | solution.py:34
  91.8 0.8 copy-start.2
  92.6 1.8 copy-start.4
  95.6 80.5 %copy-start.1 = (bf16[1,256,4,4,128]{1,4,3,2,0:T(8,128)(2,1)S(1)}, bf16[1,256,4,4,128]{1,4,3,2,0:T(8,128)(2,1)}, u32[]{:S(2)}) copy-start(bf16[1,256,4,4,128]{1,4,3,2,0:T(8,128)(2,1)} %fusion.33) | copy-start | bytes 3145732
  186.6 4.2 %collective-permute-start = (bf16[2,1,256,4,128]{4,2,3,1,0:T(8,128)(2,1)}, bf16[2,1,256,4,128]{4,2,3,1,0:T(8,128)(2,1)S(1)}, u32[]{:S(2)}, u32[]{:S(2)}) collective-permute-start(bf16[2,1,256,4,128]{4,2,3,1,0:T(8,128)(2,1)} %get-tuple-element.369), channel_id=1, source_target_pairs={{0,4},{4,8},{8,12},{12,16},{16,20},{20,24},{24,28},{1,5},{5,9},{9,... | collective-permute-start | bytes 1572872 | tf_op jit(solution)/shard_map/while/body/eval_jaxpr/ppermute | solution.py:12
  198.1 10.7 %collective-permute-start = (bf16[2,1,256,4,128]{4,2,3,1,0:T(8,128)(2,1)}, bf16[2,1,256,4,128]{4,2,3,1,0:T(8,128)(2,1)S(1)}, u32[]{:S(2)}, u32[]{:S(2)}) collective-permute-start(bf16[2,1,256,4,128]{4,2,3,1,0:T(8,128)(2,1)} %get-tuple-element.369), channel_id=1, source_target_pairs={{0,4},{4,8},{8,12},{12,16},{16,20},{20,24},{24,28},{1,5},{5,9},{9,... | collective-permute-start | bytes 1572872 | tf_op jit(solution)/shard_map/while/body/eval_jaxpr/ppermute | solution.py:12
  209.6 17.2 %collective-permute-start = (bf16[2,1,256,4,128]{4,2,3,1,0:T(8,128)(2,1)}, bf16[2,1,256,4,128]{4,2,3,1,0:T(8,128)(2,1)S(1)}, u32[]{:S(2)}, u32[]{:S(2)}) collective-permute-start(bf16[2,1,256,4,128]{4,2,3,1,0:T(8,128)(2,1)} %get-tuple-element.369), channel_id=1, source_target_pairs={{0,4},{4,8},{8,12},{12,16},{16,20},{20,24},{24,28},{1,5},{5,9},{9,... | collective-permute-start | bytes 1572872 | tf_op jit(solution)/shard_map/while/body/eval_jaxpr/ppermute | solution.py:12
  234.1 10.7 %collective-permute-start = (bf16[2,1,256,4,128]{4,2,3,1,0:T(8,128)(2,1)}, bf16[2,1,256,4,128]{4,2,3,1,0:T(8,128)(2,1)S(1)}, u32[]{:S(2)}, u32[]{:S(2)}) collective-permute-start(bf16[2,1,256,4,128]{4,2,3,1,0:T(8,128)(2,1)} %get-tuple-element.369), channel_id=1, source_target_pairs={{0,4},{4,8},{8,12},{12,16},{16,20},{20,24},{24,28},{1,5},{5,9},{9,... | collective-permute-start | bytes 1572872 | tf_op jit(solution)/shard_map/while/body/eval_jaxpr/ppermute | solution.py:12
  252.1 10.7 %collective-permute-start = (bf16[2,1,256,4,128]{4,2,3,1,0:T(8,128)(2,1)}, bf16[2,1,256,4,128]{4,2,3,1,0:T(8,128)(2,1)S(1)}, u32[]{:S(2)}, u32[]{:S(2)}) collective-permute-start(bf16[2,1,256,4,128]{4,2,3,1,0:T(8,128)(2,1)} %get-tuple-element.369), channel_id=1, source_target_pairs={{0,4},{4,8},{8,12},{12,16},{16,20},{20,24},{24,28},{1,5},{5,9},{9,... | collective-permute-start | bytes 1572872 | tf_op jit(solution)/shard_map/while/body/eval_jaxpr/ppermute | solution.py:12
  270.1 10.7 %collective-permute-start = (bf16[2,1,256,4,128]{4,2,3,1,0:T(8,128)(2,1)}, bf16[2,1,256,4,128]{4,2,3,1,0:T(8,128)(2,1)S(1)}, u32[]{:S(2)}, u32[]{:S(2)}) collective-permute-start(bf16[2,1,256,4,128]{4,2,3,1,0:T(8,128)(2,1)} %get-tuple-element.369), channel_id=1, source_target_pairs={{0,4},{4,8},{8,12},{12,16},{16,20},{20,24},{24,28},{1,5},{5,9},{9,... | collective-permute-start | bytes 1572872 | tf_op jit(solution)/shard_map/while/body/eval_jaxpr/ppermute | solution.py:12
  288.2 10.7 %collective-permute-start = (bf16[2,1,256,4,128]{4,2,3,1,0:T(8,128)(2,1)}, bf16[2,1,256,4,128]{4,2,3,1,0:T(8,128)(2,1)S(1)}, u32[]{:S(2)}, u32[]{:S(2)}) collective-permute-start(bf16[2,1,256,4,128]{4,2,3,1,0:T(8,128)(2,1)} %get-tuple-element.369), channel_id=1, source_target_pairs={{0,4},{4,8},{8,12},{12,16},{16,20},{20,24},{24,28},{1,5},{5,9},{9,... | collective-permute-start | bytes 1572872 | tf_op jit(solution)/shard_map/while/body/eval_jaxpr/ppermute | solution.py:12
Sparse Core Ops, SparseCore 0:
  8.9 79.3 all-gather.2
  89.9 79.2 all-gather.4
where the time goes:
time: 319 us; the launch traced here: 317 us
  waiting for transfers between devices  200 us (63%)
  matrix products  51.6 us (16%)
  local copies, waits for them, and re-layouts  20.3 us (6%)
  other arithmetic  17.9 us (6%)
  between operations  14.2 us (4%)
  starting transfers between devices  9 us (3%)
  loops' own time  4.89 us (2%)
    all_gather x1, waiting for transfers between devices, shards(): lax.all_gather(value_weight, 'fsdp', axis=0, tiled=True)  73.7 us
    all_gather x1, waiting for transfers between devices, shards(): key_sums = add_rows(lax.all_gather(key_weight, 'fsdp', axis=0, tiled=True))  73.4 us
    ppermute x7, waiting for transfers between devices, shifted(): lax.ppermute(value, axis, [(source, source + steps) for source in range(l...  51.1 us
    dot_general x7, matrix products, accumulate(): jnp.einsum('bkgqp,bpkd->bkgqd', weights.astype(jnp.bfloat16), value_piece...  28.5 us
    dot_general x7, matrix products, accumulate(): jnp.einsum('bqkgd,bpkd->bkgqp', scaled_q, key_piece, preferred_element_ty...  15.6 us
    reduce_or x8, other arithmetic, attend_when(): jnp.any(allow_table > 0)  10.9 us
    ppermute x7, starting transfers between devices, shifted(): lax.ppermute(value, axis, [(source, source + steps) for source in range(l...  8.96 us
    dot_general x2, matrix products, add_rows(): return jnp.dot(flat_rows, piece, preferred_element_type=jnp.float32)  7.55 us
  transfers between devices with their start and end apart: 9, of which 9 were waited for; matrix products, arithmetic and copies ran while one was open for 7% of the time, Pallas kernels for 0%

commit v1 on v0

v1 whole, which is shorter than its diff:
```python
import functools
import math

import jax
import jax.numpy as jnp
from jax import lax
from jax.experimental import pallas as pl
from jax.experimental.pallas import tpu as pltpu
from jax.sharding import PartitionSpec as P

MESH = pl.DeviceIdType.MESH


def flip(value, mask):
    bit = 1
    while bit <= mask:
        if mask & bit:
            value = value + bit - 2 * bit * lax.rem(lax.div(value, bit), 2)
        bit *= 2
    return value


def kernel(
    n_fsdp, n_chips, groups, hs_ref, mask_ref, gain_ref, hid_in, q_in, kw_in, vw_in, out_ref,
    wbuf, hid, qraw, qs, kvb, psum, acc, obuf, mbuf,
    loc_sem, sib_s, sib_r, zs, zr, xs, xr, ys, yr, fxs, fxr, fys, fyr, ks, kr,
):
    n_y = n_chips // 2
    tokens, width = hid_in.shape
    depth = kw_in.shape[0]
    half = kw_in.shape[1] // 2
    head = gain_ref.shape[1]
    frames, n_key_frames = mask_ref.shape
    frame = tokens // frames
    chip_rows = 2 * tokens
    chip_frames = 2 * frames
    kv_heads = half // head
    q_half = q_in.shape[1] // 2
    quarter = depth // n_chips

    z = lax.axis_index("fsdp")
    spot = lax.axis_index("ctx")
    chip = lax.div(spot, 2)
    core = lax.rem(spot, 2)
    y = lax.div(chip, 2)
    x = lax.rem(chip, 2)
    sibling = 1 - core

    def dev(to_chip, to_core, to_z):
        return (to_chip * 2 + to_core, to_z)

    x_chip = y * 2 + 1 - x

    def y_chip(k, column=None):
        return lax.rem(y + k, n_y) * 2 + (x if column is None else column)

    me_sib = dev(chip, sibling, z)
    x_dev = dev(x_chip, core, z)

    own_rows = pl.ds(pl.multiple_of(core * tokens, tokens), tokens)
    sib_rows = pl.ds(pl.multiple_of(sibling * tokens, tokens), tokens)
    own_half = pl.ds(pl.multiple_of(core * half, half), half)
    own_q = pl.ds(pl.multiple_of(core * q_half, q_half), q_half)
    sib_q = pl.ds(pl.multiple_of(sibling * q_half, q_half), q_half)

    local = [
        pltpu.make_async_copy(hid_in, hid.at[own_rows, :], loc_sem.at[0]),
        pltpu.make_async_copy(q_in.at[:, own_q], qraw.at[own_rows, :], loc_sem.at[1]),
        pltpu.make_async_copy(kw_in.at[:, own_half], wbuf.at[z, 0], loc_sem.at[2]),
        pltpu.make_async_copy(vw_in.at[:, own_half], wbuf.at[z, 1], loc_sem.at[3]),
    ]
    for copy in local:
        copy.start()

    partners = [me_sib]
    partners += [dev(chip, core, flip(z, j)) for j in range(1, n_fsdp)]
    partners += [dev(lax.rem(chip + d, n_chips), core, z) for d in range(1, n_chips)]
    barrier = pltpu.get_barrier_semaphore()
    for partner in partners:
        pl.semaphore_signal(barrier, inc=1, device_id=partner, device_id_type=MESH)
    for f in range(frames):
        for k in range(n_key_frames):
            seen = jnp.where(mask_ref[f, k] > 0, 1.0, 0.0).astype(jnp.float32)
            mbuf[core, f, pl.ds(k, 1), :] = jnp.full((1, head), seen, jnp.float32)
    pl.semaphore_wait(barrier, len(partners))

    def remote(src, dst, send, recv, to):
        return pltpu.make_async_remote_copy(
            src_ref=src, dst_ref=dst, send_sem=send, recv_sem=recv, device_id=to, device_id_type=MESH
        )

    def rows_of(q, part=None):
        if part is None:
            return pl.ds(pl.multiple_of(q * quarter, quarter), quarter)
        size = quarter // 2
        return pl.ds(pl.multiple_of(q * quarter + part * size, size), size)

    def piece(j, kv, q, part=None):
        return wbuf.at[flip(z, j), kv, rows_of(q, part), :]

    def z_copy(kv, j):
        source = (kw_in, vw_in)[kv].at[rows_of(chip), own_half]
        landing = wbuf.at[z, kv, rows_of(chip), :]
        return remote(source, landing, zs.at[kv, j], zr.at[kv, j], dev(chip, core, flip(z, j)))

    def z_land(kv, j):
        land = piece(j, kv, chip)
        return remote(land, land, zs.at[kv, j], zr.at[kv, j], dev(chip, core, flip(z, j)))

    def x_copy(kv, j, q):
        land = piece(j, kv, q)
        return remote(land, land, xs.at[kv, j], xr.at[kv, j], x_dev)

    def y_copy(kv, j, k, q):
        land = piece(j, kv, q)
        return remote(land, land, ys.at[kv, j, k], yr.at[kv, j, k], dev(y_chip(k), core, z))

    def fx_copy(kv, j, k, q):
        land = piece(j, kv, q, 0)
        return remote(land, land, fxs.at[kv, j, k], fxr.at[kv, j, k], x_dev)

    def fy_copy(kv, j, k, q):
        land = piece(j, kv, q, 1)
        return remote(land, land, fys.at[kv, j, k], fyr.at[kv, j, k], dev(y_chip(k), core, z))

    others = list(range(1, n_fsdp))
    back = lambda k: n_y - k
    waits = []

    def go(copy):
        copy.start()
        waits.append(copy)

    for kv in range(2):
        for j in others:
            go(z_copy(kv, j))
        if kv == 0:
            sib = [
                remote(hid_in, hid.at[own_rows, :], sib_s.at[0], sib_r.at[0], me_sib),
                remote(q_in.at[:, sib_q], qraw.at[own_rows, :], sib_s.at[1], sib_r.at[1], me_sib),
                remote(mbuf.at[core], mbuf.at[core], sib_s.at[2], sib_r.at[2], me_sib),
            ]
            for copy in sib:
                go(copy)

    def sib_land(n):
        land = (hid.at[sib_rows, :], qraw.at[sib_rows, :], mbuf.at[sibling])[n]
        return remote(land, land, sib_s.at[n], sib_r.at[n], me_sib)

    def stage1(kv, j):
        z_land(kv, j).wait_recv()
        go(x_copy(kv, j, chip))
        for k in range(1, n_y):
            go(y_copy(kv, j, k, chip))

    def stage2(kv, j):
        x_copy(kv, j, x_chip).wait_recv()
        for k in range(1, n_y):
            go(fy_copy(kv, j, k, x_chip))
        for k in range(1, n_y):
            source = y_chip(back(k))
            y_copy(kv, j, k, source).wait_recv()
            go(fx_copy(kv, j, k, source))

    def multiply(kv, j, first):
        zz = flip(z, j)
        cols = pl.ds(pl.multiple_of(zz * depth, depth), depth)
        part = jnp.dot(hid[:, cols], wbuf[zz, kv], preferred_element_type=jnp.float32)
        if first:
            psum[...] = part
        else:
            psum[...] += part

    def stage3(kv, j):
        for k in range(1, n_y):
            source = y_chip(back(k), 1 - x)
            fx_copy(kv, j, k, source).wait_recv()
            fy_copy(kv, j, k, source).wait_recv()
        multiply(kv, j, False)

    def kv_copy(kv, d, to):
        return remote(kvb.at[chip, kv], kvb.at[chip, kv], ks.at[kv, d], kr.at[kv, d], dev(to, core, z))

    def send_kv(kv):
        for d in range(1, n_chips):

            @pl.when(chip + d < n_chips)
            def _():
                kv_copy(kv, d, chip + d).start()

    for copy in local:
        copy.wait()
    for n in range(3):
        sib_land(n).wait_recv()

    def scale_queries(h, carried):
        kv_head = lax.div(h, groups)
        g = lax.rem(h, groups)
        factor = hs_ref[core * (kv_heads * groups) + h] * (1.0 / math.sqrt(head))
        cols = pl.ds(pl.multiple_of(h * head, head), head)
        for f in range(chip_frames):
            q = qraw[f * frame : (f + 1) * frame, cols].astype(jnp.float32)
            mean = jnp.mean(q * q, axis=-1, keepdims=True)
            q = q * lax.rsqrt(mean + 1e-6) * factor
            qs[kv_head, f, pl.ds(pl.multiple_of(g * frame, frame), frame), :] = q.astype(jnp.bfloat16)
        return carried

    def finish(kv):
        for h in range(kv_heads):
            vecs = psum[:, h * head : (h + 1) * head]
            if kv == 0:
                mean = jnp.mean(vecs * vecs, axis=-1, keepdims=True)
                vecs = vecs * lax.rsqrt(mean + 1e-6) * gain_ref[...]
            kvb[chip, kv, h] = vecs.astype(jnp.bfloat16)
        send_kv(kv)

    units = [(kv, j) for kv in range(2) for j in others]
    multiply(0, 0, True)
    for t in range(len(units) + 2):
        if t < len(units):
            stage1(*units[t])
        if t == 0:
            lax.fori_loop(0, kv_heads * groups, scale_queries, 0)
        if 0 <= t - 1 < len(units):
            stage2(*units[t - 1])
        if t >= 2:
            stage3(*units[t - 2])
            if t - 2 == len(others) - 1:
                finish(0)
                multiply(1, 0, True)
    finish(1)

    def attend(source, first):
        def body(step, carried):
            h = lax.div(step, chip_frames)
            f = lax.rem(step, chip_frames)
            scores = lax.dot_general(
                qs[h, f], kvb[source, 0, h], (((1,), (1,)), ((), ())), preferred_element_type=jnp.float32
            )
            weights = jnp.exp(scores).astype(jnp.bfloat16)
            values = []
            for k in range(chip_frames):
                seen = mbuf[lax.div(f, frames), lax.rem(f, frames), pl.ds(source * chip_frames + k, 1), :]
                seen = jnp.broadcast_to(seen, (frame, head)).astype(jnp.bfloat16)
                value = kvb[source, 1, h, k * frame : (k + 1) * frame, :] * seen
                values.append(jnp.concatenate([value, seen], axis=1))
            both = jnp.dot(weights, jnp.concatenate(values, axis=0), preferred_element_type=jnp.float32)
            if first:
                acc[step] = both
            else:
                acc[step] += both
            return carried

        lax.fori_loop(0, kv_heads * chip_frames, body, 0)

    attend(chip, True)
    for d in range(1, n_chips):

        @pl.when(chip >= d)
        def _():
            source = chip - d
            for kv in range(2):
                land = kvb.at[source, kv]
                remote(land, land, ks.at[kv, d], kr.at[kv, d], me_sib).wait_recv()
            attend(source, False)

    def divide(f, carried):
        for h in range(kv_heads):
            both = acc[h * chip_frames + f]
            ratio = (both[:, :head] / both[:, head:]).astype(jnp.bfloat16)
            for g in range(groups):
                at = (h * groups + g) * head
                obuf[pl.ds(pl.multiple_of(f * frame, frame), frame), at : at + head] = ratio[
                    g * frame : (g + 1) * frame
                ]
        return carried

    lax.fori_loop(0, chip_frames, divide, 0)
    keep = pltpu.make_async_copy(obuf.at[own_rows, :], out_ref.at[:, own_q], loc_sem.at[4])
    give = remote(obuf.at[sib_rows, :], out_ref.at[:, own_q], sib_s.at[3], sib_r.at[3], me_sib)
    keep.start()
    give.start()

    for copy in waits:
        copy.wait_send()
    for kv in range(2):
        for d in range(1, n_chips):

            @pl.when(chip + d < n_chips)
            def _():
                kv_copy(kv, d, chip + d).wait_send()

    keep.wait()
    give.wait_send()
    remote(out_ref.at[:, sib_q], out_ref.at[:, sib_q], sib_s.at[3], sib_r.at[3], me_sib).wait_recv()


def shards(hidden, queries, key_weight, value_weight, key_gain, head_scale, block_mask):
    n_fsdp = lax.axis_size("fsdp")
    n_chips = lax.axis_size("ctx") // 2
    n_y = n_chips // 2
    _, tokens, width = hidden.shape
    q_width = queries.shape[2]
    depth, kv_width = key_weight.shape
    head = key_gain.shape[0]
    heads = head_scale.shape[0]
    half = kv_width // 2
    kv_heads = half // head
    groups = heads // (2 * kv_heads)
    frames, n_key_frames = block_mask.shape[1:]
    frame = tokens // frames
    hbm = pl.BlockSpec(memory_space=pl.ANY)
    smem = pl.BlockSpec(memory_space=pltpu.SMEM)
    dma = pltpu.SemaphoreType.DMA
    out = pl.pallas_call(
        functools.partial(kernel, n_fsdp, n_chips, groups),
        out_shape=jax.ShapeDtypeStruct((tokens, q_width), jnp.bfloat16),
        in_specs=[smem, smem, pl.BlockSpec(memory_space=pltpu.VMEM), hbm, hbm, hbm, hbm],
        out_specs=hbm,
        scratch_shapes=[
            pltpu.VMEM((n_fsdp, 2, depth, half), jnp.bfloat16),
            pltpu.VMEM((2 * tokens, width), jnp.bfloat16),
            pltpu.VMEM((2 * tokens, q_width // 2), jnp.bfloat16),
            pltpu.VMEM((kv_heads, 2 * frames, groups * frame, head), jnp.bfloat16),
            pltpu.VMEM((n_chips, 2, kv_heads, 2 * tokens, head), jnp.bfloat16),
            pltpu.VMEM((2 * tokens, half), jnp.float32),
            pltpu.VMEM((kv_heads * 2 * frames, groups * frame, 2 * head), jnp.float32),
            pltpu.VMEM((2 * tokens, q_width // 2), jnp.bfloat16),
            pltpu.VMEM((2, frames, n_key_frames, head), jnp.float32),
            dma((5,)),
            dma((4,)),
            dma((4,)),
            dma((2, n_fsdp)),
            dma((2, n_fsdp)),
            dma((2, n_fsdp)),
            dma((2, n_fsdp)),
            dma((2, n_fsdp, n_y)),
            dma((2, n_fsdp, n_y)),
            dma((2, n_fsdp, n_y)),
            dma((2, n_fsdp, n_y)),
            dma((2, n_fsdp, n_y)),
            dma((2, n_fsdp, n_y)),
            dma((2, n_chips)),
            dma((2, n_chips)),
        ],
        compiler_params=pltpu.CompilerParams(
            collective_id=0, has_side_effects=True, vmem_limit_bytes=48 * 1024 * 1024
        ),
    )(
        head_scale, block_mask[0], key_gain.reshape(1, head), hidden[0], queries[0], key_weight, value_weight
    )
    return out[None]


def solution(mesh):
    placed = (
        P("fsdp", "ctx", None),
        P("fsdp", "ctx", None),
        P("fsdp", None),
        P("fsdp", None),
        P(),
        P(),
        P("fsdp", "ctx", None),
    )
    return jax.shard_map(
        shards, mesh=mesh, in_specs=placed, out_specs=P("fsdp", "ctx", None), check_vma=False
    )
```

time: 319 us -> 82.5 us (0.26)
  waiting for transfers between devices: 200 us -> 0 us
  Pallas kernels: 0 us -> 75.6 us
  matrix products: 51.6 us -> 0 us
  other arithmetic: 17.9 us -> 0 us
  between operations: 14.2 us -> 0.02 us
  local copies, waits for them, and re-layouts: 20.3 us -> 6.63 us
  starting transfers between devices: 9 us -> 0 us
  loops' own time: 4.89 us -> 0 us
    all_gather x2 -> x0, waiting for transfers between devices: 147 us -> none  [the longest x1 73.7 us: shards(): lax.all_gather(value_weight, 'fsdp', axis=0, tiled=True)]
    pallas_call x0 -> x1, Pallas kernels: none -> 75.6 us  [shards(): pl.pallas_call(functools.partial(kernel, n_fsdp, n_chips, groups), out_sh...]
    dot_general x16 -> x0, matrix products: 51.6 us -> none  [the longest x7 28.5 us: accumulate(): jnp.einsum('bkgqp,bpkd->bkgqd', weights.astype(jnp.bfloat16), value_piece...]
    ppermute x7 -> x0, waiting for transfers between devices: 51.1 us -> none  [shifted(): lax.ppermute(value, axis, [(source, source + steps) for source in range(l...]
    reduce_or x8 -> x0, other arithmetic: 10.9 us -> none  [attend_when(): jnp.any(allow_table > 0)]
    ppermute x7 -> x0, starting transfers between devices: 8.96 us -> none  [shifted(): lax.ppermute(value, axis, [(source, source + steps) for source in range(l...]
    while x8 -> x0, local copies, waits for them, and re-layouts: 7.87 us -> none
    another operation x9 -> x0, loops' own time: 4.89 us -> none  [the longest x1 4.72 us: shards(): result = lax.fori_loop(1, ctx_count, relay_step, (result, stacked))[0]]
  transfers between devices with their start and end apart: 9 -> 0, of which waited for: 9 -> 0; matrix products, arithmetic and copies ran while one was open for 7% -> 0% of each run, Pallas kernels for 0% -> 0%
where the time goes in v1:
time: 82.5 us; the launch traced here: 82.2 us
  Pallas kernels  75.6 us (92%)
  local copies, waits for them, and re-layouts  6.63 us (8%)
    pallas_call x1, Pallas kernels, shards(): pl.pallas_call(functools.partial(kernel, n_fsdp, n_chips, groups), out_sh...  75.6 us
    unnamed x13, local copies, waits for them, and re-layouts  6.63 us

profile of v1, /device:TPU:15, one launch (start us, length us, event | category | flops | bytes accessed | tf_op | source)
XLA Modules:
  0.0 82.2 jit_solution(14339552608703922409)
XLA Ops:
  0.0 0.0 copy-start
  0.0 1.2 %copy-done = bf16[1,256,2048]{2,1,0:T(8,128)(2,1)S(1)} copy-done((bf16[1,256,2048]{2,1,0:T(8,128)(2,1)S(1)}, bf16[1,256,2048]{2,1,0:T(8,128)(2,1)}, u32[]{:S(2)}) %copy-start) | copy-done | bytes 1048600
  1.2 0.0 copy-start.1
  1.2 1.2 %copy-done.1 = bf16[1024,512]{1,0:T(8,128)(2,1)S(1)} copy-done((bf16[1024,512]{1,0:T(8,128)(2,1)S(1)}, bf16[1024,512]{1,0:T(8,128)(2,1)}, u32[]{:S(2)}) %copy-start.1) | copy-done | bytes 1048600
  2.5 0.0 copy-start.2
  2.5 1.2 %copy-done.2 = bf16[1024,512]{1,0:T(8,128)(2,1)S(1)} copy-done((bf16[1024,512]{1,0:T(8,128)(2,1)S(1)}, bf16[1024,512]{1,0:T(8,128)(2,1)}, u32[]{:S(2)}) %copy-start.2) | copy-done | bytes 1048600
  3.7 0.0 copy-start.3
  3.7 0.7 copy-done.3
  4.4 0.0 copy-start.4
  4.4 0.7 copy-done.4
  5.0 0.0 copy-start.5
  5.0 0.7 copy-done.5
  5.7 75.6 %shard_map.73 = bf16[256,2048]{1,0:T(8,128)(2,1)S(1)} custom-call(f32[16]{0:T(128)S(1)} %copy-done.4, s32[2,16]{1,0:T(2,128)S(1)} %bitcast.7, f32[1,128]{1,0:T(1,128)S(1)} %bitcast.8, bf16[256,4096]{1,0:T(8,128)(2,1)} %bitcast.9, bf16[256,2048]{1,0:T(8,128)(2,1)S(1)} %bitcast.6, bf16[1024,512]{1,0:T(8,128)(2,1)S(1)} %copy-done.1, bf16[1024,512]{1,0:T(8,128)(2,1)S(1)} %copy-done.2), custom_call_target="tpu_custom_call" | custom-call | tf_op jit(solution)/shard_map/pallas_call | solution.py:315
  81.2 1.0 %copy.9 = bf16[1,256,2048]{2,1,0:T(8,128)(2,1)} copy(bf16[1,256,2048]{2,1,0:T(8,128)(2,1)S(1)} %bitcast.5) | data formatting | bytes 2097152
Async XLA Ops:
  0.0 1.2 %copy-start = (bf16[1,256,2048]{2,1,0:T(8,128)(2,1)S(1)}, bf16[1,256,2048]{2,1,0:T(8,128)(2,1)}, u32[]{:S(2)}) copy-start(bf16[1,256,2048]{2,1,0:T(8,128)(2,1)} %param.8) | copy-start | bytes 3145732
  1.2 1.2 %copy-start.1 = (bf16[1024,512]{1,0:T(8,128)(2,1)S(1)}, bf16[1024,512]{1,0:T(8,128)(2,1)}, u32[]{:S(2)}) copy-start(bf16[1024,512]{1,0:T(8,128)(2,1)} %kw_in.1) | copy-start | bytes 3145732
  2.5 1.2 %copy-start.2 = (bf16[1024,512]{1,0:T(8,128)(2,1)S(1)}, bf16[1024,512]{1,0:T(8,128)(2,1)}, u32[]{:S(2)}) copy-start(bf16[1024,512]{1,0:T(8,128)(2,1)} %vw_in.1) | copy-start | bytes 3145732
  3.7 0.7 copy-start.3
  4.4 0.7 copy-start.4
  5.0 0.7 copy-start.5

commit v2 on v1

--- a/solution.py
+++ b/solution.py
@@ -11,18 +11,12 @@
 MESH = pl.DeviceIdType.MESH
 
 
-def flip(value, mask):
-    bit = 1
-    while bit <= mask:
-        if mask & bit:
-            value = value + bit - 2 * bit * lax.rem(lax.div(value, bit), 2)
-        bit *= 2
-    return value
+DIAGONAL_ALONG_Z = (False, False)
 
 
 def kernel(
     n_fsdp, n_chips, groups, hs_ref, mask_ref, gain_ref, hid_in, q_in, kw_in, vw_in, out_ref,
-    wbuf, hid, qraw, qs, kvb, psum, acc, obuf, mbuf,
+    wbuf, hid, qraw, qs, kvb, psum, pbuf, acc, obuf, mbuf,
     loc_sem, sib_s, sib_r, zs, zr, xs, xr, ys, yr, fxs, fxr, fys, fyr, ks, kr,
 ):
     n_y = n_chips // 2
@@ -73,11 +67,21 @@
         copy.start()
 
     partners = [me_sib]
-    partners += [dev(chip, core, flip(z, j)) for j in range(1, n_fsdp)]
+    partners += [dev(chip, core, lax.rem(z + j, n_fsdp)) for j in range(1, n_fsdp)]
     partners += [dev(lax.rem(chip + d, n_chips), core, z) for d in range(1, n_chips)]
     barrier = pltpu.get_barrier_semaphore()
     for partner in partners:
         pl.semaphore_signal(barrier, inc=1, device_id=partner, device_id_type=MESH)
+
+    def has_next(up):
+        return z + 1 < n_fsdp if up else z >= 1
+
+    def has_unit(up, d):
+        return z >= d if up else z + d < n_fsdp
+
+    def next_dev(up):
+        return dev(chip, core, z + 1 if up else z - 1)
+
     for f in range(frames):
         for k in range(n_key_frames):
             seen = jnp.where(mask_ref[f, k] > 0, 1.0, 0.0).astype(jnp.float32)
@@ -95,75 +99,97 @@
         size = quarter // 2
         return pl.ds(pl.multiple_of(q * quarter + part * size, size), size)
 
-    def piece(j, kv, q, part=None):
-        return wbuf.at[flip(z, j), kv, rows_of(q, part), :]
-
-    def z_copy(kv, j):
-        source = (kw_in, vw_in)[kv].at[rows_of(chip), own_half]
-        landing = wbuf.at[z, kv, rows_of(chip), :]
-        return remote(source, landing, zs.at[kv, j], zr.at[kv, j], dev(chip, core, flip(z, j)))
-
-    def z_land(kv, j):
-        land = piece(j, kv, chip)
-        return remote(land, land, zs.at[kv, j], zr.at[kv, j], dev(chip, core, flip(z, j)))
-
-    def x_copy(kv, j, q):
-        land = piece(j, kv, q)
-        return remote(land, land, xs.at[kv, j], xr.at[kv, j], x_dev)
-
-    def y_copy(kv, j, k, q):
-        land = piece(j, kv, q)
-        return remote(land, land, ys.at[kv, j, k], yr.at[kv, j, k], dev(y_chip(k), core, z))
-
-    def fx_copy(kv, j, k, q):
-        land = piece(j, kv, q, 0)
-        return remote(land, land, fxs.at[kv, j, k], fxr.at[kv, j, k], x_dev)
-
-    def fy_copy(kv, j, k, q):
-        land = piece(j, kv, q, 1)
-        return remote(land, land, fys.at[kv, j, k], fyr.at[kv, j, k], dev(y_chip(k), core, z))
-
-    others = list(range(1, n_fsdp))
+    def piece(zz, kv, q, part=None):
+        return wbuf.at[zz, kv, rows_of(q, part), :]
+
     back = lambda k: n_y - k
-    waits = []
-
-    def go(copy):
+
+    def z_parts(kv):
+        quarters = [chip]
+        if DIAGONAL_ALONG_Z[kv]:
+            quarters += [y_chip(k, 1 - x) for k in range(1, n_y)]
+        return list(enumerate(quarters))
+
+    def z_copy(kv, zz, n, q, up, first=False):
+        land = piece(zz, kv, q)
+        source = (kw_in, vw_in)[kv].at[rows_of(q), own_half] if first else land
+        return remote(source, land, zs.at[up, kv, zz, n], zr.at[kv, zz, n], next_dev(up))
+
+    def x_copy(kv, zz, q):
+        land = piece(zz, kv, q)
+        return remote(land, land, xs.at[kv, zz], xr.at[kv, zz], x_dev)
+
+    def y_copy(kv, zz, k, q):
+        land = piece(zz, kv, q)
+        return remote(land, land, ys.at[kv, zz, k], yr.at[kv, zz, k], dev(y_chip(k), core, z))
+
+    def fx_copy(kv, zz, k, q):
+        land = piece(zz, kv, q, 0)
+        return remote(land, land, fxs.at[kv, zz, k], fxr.at[kv, zz, k], x_dev)
+
+    def fy_copy(kv, zz, k, q):
+        land = piece(zz, kv, q, 1)
+        return remote(land, land, fys.at[kv, zz, k], fyr.at[kv, zz, k], dev(y_chip(k), core, z))
+
+    def first_send(kv):
+        for up in (True, False):
+
+            @pl.when(has_next(up))
+            def _():
+                for n, q in z_parts(kv):
+                    z_copy(kv, z, n, q, int(up), True).start()
+
+    first_send(0)
+    sib = [
+        remote(hid_in, hid.at[own_rows, :], sib_s.at[0], sib_r.at[0], me_sib),
+        remote(q_in.at[:, sib_q], qraw.at[own_rows, :], sib_s.at[1], sib_r.at[1], me_sib),
+        remote(mbuf.at[core], mbuf.at[core], sib_s.at[2], sib_r.at[2], me_sib),
+    ]
+    for copy in sib:
         copy.start()
-        waits.append(copy)
-
-    for kv in range(2):
-        for j in others:
-            go(z_copy(kv, j))
-        if kv == 0:
-            sib = [
-                remote(hid_in, hid.at[own_rows, :], sib_s.at[0], sib_r.at[0], me_sib),
-                remote(q_in.at[:, sib_q], qraw.at[own_rows, :], sib_s.at[1], sib_r.at[1], me_sib),
-                remote(mbuf.at[core], mbuf.at[core], sib_s.at[2], sib_r.at[2], me_sib),
-            ]
-            for copy in sib:
-                go(copy)
 
     def sib_land(n):
         land = (hid.at[sib_rows, :], qraw.at[sib_rows, :], mbuf.at[sibling])[n]
         return remote(land, land, sib_s.at[n], sib_r.at[n], me_sib)
 
-    def stage1(kv, j):
-        z_land(kv, j).wait_recv()
-        go(x_copy(kv, j, chip))
-        for k in range(1, n_y):
-            go(y_copy(kv, j, k, chip))
-
-    def stage2(kv, j):
-        x_copy(kv, j, x_chip).wait_recv()
-        for k in range(1, n_y):
-            go(fy_copy(kv, j, k, x_chip))
-        for k in range(1, n_y):
-            source = y_chip(back(k))
-            y_copy(kv, j, k, source).wait_recv()
-            go(fx_copy(kv, j, k, source))
-
-    def multiply(kv, j, first):
-        zz = flip(z, j)
+    def each_unit(d, action):
+        for up in (True, False):
+
+            @pl.when(has_unit(up, d))
+            def _():
+                action(up, z - d if up else z + d)
+
+    def stage1(kv, d):
+        def action(up, zz):
+            for n, q in z_parts(kv):
+                z_copy(kv, zz, n, q, int(up)).wait_recv()
+
+                @pl.when(has_next(up))
+                def _():
+                    z_copy(kv, zz, n, q, int(up)).start()
+
+                if n == 0:
+                    x_copy(kv, zz, chip).start()
+                    for k in range(1, n_y):
+                        y_copy(kv, zz, k, chip).start()
+
+        each_unit(d, action)
+
+    def stage2(kv, d):
+        def action(up, zz):
+            x_copy(kv, zz, x_chip).wait_recv()
+            if not DIAGONAL_ALONG_Z[kv]:
+                for k in range(1, n_y):
+                    fy_copy(kv, zz, k, x_chip).start()
+            for k in range(1, n_y):
+                source = y_chip(back(k))
+                y_copy(kv, zz, k, source).wait_recv()
+                if not DIAGONAL_ALONG_Z[kv]:
+                    fx_copy(kv, zz, k, source).start()
+
+        each_unit(d, action)
+
+    def multiply(kv, zz, first):
         cols = pl.ds(pl.multiple_of(zz * depth, depth), depth)
         part = jnp.dot(hid[:, cols], wbuf[zz, kv], preferred_element_type=jnp.float32)
         if first:
@@ -171,12 +197,44 @@
         else:
             psum[...] += part
 
-    def stage3(kv, j):
-        for k in range(1, n_y):
-            source = y_chip(back(k), 1 - x)
-            fx_copy(kv, j, k, source).wait_recv()
-            fy_copy(kv, j, k, source).wait_recv()
-        multiply(kv, j, False)
+    def stage3(kv, d):
+        def action(up, zz):
+            if not DIAGONAL_ALONG_Z[kv]:
+                for k in range(1, n_y):
+                    source = y_chip(back(k), 1 - x)
+                    fx_copy(kv, zz, k, source).wait_recv()
+                    fy_copy(kv, zz, k, source).wait_recv()
+            multiply(kv, zz, False)
+
+        each_unit(d, action)
+
+    def finish_sends():
+        for copy in sib:
+            copy.wait_send()
+        for kv in range(2):
+            for up in (True, False):
+
+                @pl.when(has_next(up))
+                def _():
+                    for n, q in z_parts(kv):
+                        z_copy(kv, z, n, q, int(up), True).wait_send()
+
+            def action(up, zz):
+                for n, q in z_parts(kv):
+
+                    @pl.when(has_next(up))
+                    def _():
+                        z_copy(kv, zz, n, q, int(up)).wait_send()
+
+                x_copy(kv, zz, chip).wait_send()
+                for k in range(1, n_y):
+                    y_copy(kv, zz, k, chip).wait_send()
+                    if not DIAGONAL_ALONG_Z[kv]:
+                        fy_copy(kv, zz, k, x_chip).wait_send()
+                        fx_copy(kv, zz, k, y_chip(back(k))).wait_send()
+
+            for d in range(1, n_fsdp):
+                each_unit(d, action)
 
     def kv_copy(kv, d, to):
         return remote(kvb.at[chip, kv], kvb.at[chip, kv], ks.at[kv, d], kr.at[kv, d], dev(to, core, z))
@@ -214,55 +272,72 @@
             kvb[chip, kv, h] = vecs.astype(jnp.bfloat16)
         send_kv(kv)
 
-    units = [(kv, j) for kv in range(2) for j in others]
-    multiply(0, 0, True)
-    for t in range(len(units) + 2):
-        if t < len(units):
-            stage1(*units[t])
-        if t == 0:
-            lax.fori_loop(0, kv_heads * groups, scale_queries, 0)
-        if 0 <= t - 1 < len(units):
-            stage2(*units[t - 1])
-        if t >= 2:
-            stage3(*units[t - 2])
-            if t - 2 == len(others) - 1:
-                finish(0)
-                multiply(1, 0, True)
-    finish(1)
-
-    def attend(source, first):
+    def score(source):
         def body(step, carried):
             h = lax.div(step, chip_frames)
             f = lax.rem(step, chip_frames)
             scores = lax.dot_general(
                 qs[h, f], kvb[source, 0, h], (((1,), (1,)), ((), ())), preferred_element_type=jnp.float32
             )
-            weights = jnp.exp(scores).astype(jnp.bfloat16)
+            pbuf[source, step] = jnp.exp(scores).astype(jnp.bfloat16)
+            return carried
+
+        lax.fori_loop(0, kv_heads * chip_frames, body, 0, unroll=2)
+
+    def mix(source, first):
+        def body(step, carried):
+            h = lax.div(step, chip_frames)
+            f = lax.rem(step, chip_frames)
             values = []
             for k in range(chip_frames):
                 seen = mbuf[lax.div(f, frames), lax.rem(f, frames), pl.ds(source * chip_frames + k, 1), :]
                 seen = jnp.broadcast_to(seen, (frame, head)).astype(jnp.bfloat16)
                 value = kvb[source, 1, h, k * frame : (k + 1) * frame, :] * seen
                 values.append(jnp.concatenate([value, seen], axis=1))
-            both = jnp.dot(weights, jnp.concatenate(values, axis=0), preferred_element_type=jnp.float32)
+            both = jnp.dot(
+                pbuf[source, step], jnp.concatenate(values, axis=0), preferred_element_type=jnp.float32
+            )
             if first:
                 acc[step] = both
             else:
                 acc[step] += both
             return carried
 
-        lax.fori_loop(0, kv_heads * chip_frames, body, 0)
-
-    attend(chip, True)
-    for d in range(1, n_chips):
-
-        @pl.when(chip >= d)
-        def _():
-            source = chip - d
-            for kv in range(2):
+        lax.fori_loop(0, kv_heads * chip_frames, body, 0, unroll=2)
+
+    def with_piece(kv, use, among=True):
+        for d in range(1, n_chips):
+
+            @pl.when(jnp.logical_and(chip >= d, among))
+            def _():
+                source = chip - d
                 land = kvb.at[source, kv]
                 remote(land, land, ks.at[kv, d], kr.at[kv, d], me_sib).wait_recv()
-            attend(source, False)
+                use(source)
+
+    units = [(kv, d) for kv in range(2) for d in range(1, n_fsdp)]
+    last = len(units) - 1
+    multiply(0, z, True)
+    for t in range(len(units) + 2):
+        if t <= last:
+            stage1(*units[t])
+        if t == 0:
+            first_send(1)
+            lax.fori_loop(0, kv_heads * groups, scale_queries, 0)
+        if 0 <= t - 1 <= last:
+            stage2(*units[t - 1])
+        if t - 1 == last:
+            with_piece(0, score, chip == n_chips - 1)
+        if t >= 2:
+            stage3(*units[t - 2])
+            if t - 2 == n_fsdp - 2:
+                finish(0)
+                multiply(1, z, True)
+                score(chip)
+    finish(1)
+    with_piece(0, score, chip < n_chips - 1)
+    mix(chip, True)
+    with_piece(1, lambda source: mix(source, False))
 
     def divide(f, carried):
         for h in range(kv_heads):
@@ -281,8 +356,7 @@
     keep.start()
     give.start()
 
-    for copy in waits:
-        copy.wait_send()
+    finish_sends()
     for kv in range(2):
         for d in range(1, n_chips):
 
@@ -309,7 +383,7 @@
     groups = heads // (2 * kv_heads)
     frames, n_key_frames = block_mask.shape[1:]
     frame = tokens // frames
-    hbm = pl.BlockSpec(memory_space=pl.ANY)
+    hbm = pl.BlockSpec(memory_space=pltpu.HBM)
     smem = pl.BlockSpec(memory_space=pltpu.SMEM)
     dma = pltpu.SemaphoreType.DMA
     out = pl.pallas_call(
@@ -324,14 +398,15 @@
             pltpu.VMEM((kv_heads, 2 * frames, groups * frame, head), jnp.bfloat16),
             pltpu.VMEM((n_chips, 2, kv_heads, 2 * tokens, head), jnp.bfloat16),
             pltpu.VMEM((2 * tokens, half), jnp.float32),
+            pltpu.VMEM((n_chips, kv_heads * 2 * frames, groups * frame, 2 * tokens), jnp.bfloat16),
             pltpu.VMEM((kv_heads * 2 * frames, groups * frame, 2 * head), jnp.float32),
             pltpu.VMEM((2 * tokens, q_width // 2), jnp.bfloat16),
             pltpu.VMEM((2, frames, n_key_frames, head), jnp.float32),
             dma((5,)),
             dma((4,)),
             dma((4,)),
-            dma((2, n_fsdp)),
-            dma((2, n_fsdp)),
+            dma((2, 2, n_fsdp, n_y)),
+            dma((2, n_fsdp, n_y)),
             dma((2, n_fsdp)),
             dma((2, n_fsdp)),
             dma((2, n_fsdp, n_y)),
@@ -344,7 +419,7 @@
             dma((2, n_chips)),
         ],
         compiler_params=pltpu.CompilerParams(
-            collective_id=0, has_side_effects=True, vmem_limit_bytes=48 * 1024 * 1024
+            collective_id=0, has_side_effects=True, vmem_limit_bytes=63 * 1024 * 1024
         ),
     )(
         head_scale, block_mask[0], key_gain.reshape(1, head), hidden[0], queries[0], key_weight, value_weight

time: 82.5 us -> 71.3 us (0.86)
  Pallas kernels: 75.6 us -> 68.8 us
  local copies, waits for them, and re-layouts: 6.63 us -> 2.3 us
    pallas_call x1, Pallas kernels: 75.6 us -> 68.8 us  [shards(): pl.pallas_call(functools.partial(kernel, n_fsdp, n_chips, groups), out_sh...]
    unnamed x13 -> x1, local copies, waits for them, and re-layouts: 6.63 us -> 2.3 us
where the time goes in v2:
time: 71.3 us; the launch traced here: 71.2 us
  Pallas kernels  68.8 us (96%)
  local copies, waits for them, and re-layouts  2.3 us (3%)
    pallas_call x1, Pallas kernels, shards(): pl.pallas_call(functools.partial(kernel, n_fsdp, n_chips, groups), out_sh...  68.8 us
    unnamed x1, local copies, waits for them, and re-layouts  2.3 us

profile of v2, /device:TPU:15, one launch (start us, length us, event | category | flops | bytes accessed | tf_op | source)
XLA Modules:
  0.0 71.2 jit_solution(11337250595704783916)
XLA Ops:
  0.0 68.8 %shard_map.73 = bf16[256,2048]{1,0:T(8,128)(2,1)} custom-call(f32[16]{0:T(128)} %hs_ref.1, s32[2,16]{1,0:T(2,128)} %bitcast.8, f32[1,128]{1,0:T(1,128)} %bitcast.9, bf16[256,4096]{1,0:T(8,128)(2,1)} %bitcast.6, bf16[256,2048]{1,0:T(8,128)(2,1)} %bitcast.7, bf16[1024,512]{1,0:T(8,128)(2,1)} %kw_in.1, bf16[1024,512]{1,0:T(8,128)(2,1)} %vw_in.1), custom_call_target="tpu_custom_call" | custom-call | tf_op jit(solution)/shard_map/pallas_call | solution.py:389
  68.9 2.3 %copy.9 = bf16[1,256,2048]{2,1,0:T(8,128)(2,1)} copy(bf16[1,256,2048]{2,1,0:T(8,128)(2,1)} %bitcast.5) | data formatting | bytes 2097152
